TPU v7x, 32 devices: a whole 2x2x4 slice. The times are simulated.
32 devices in a mesh: dp: 2 (over y), row: 4 (over x, core), col: 4 (over z).
Axes of the slice: x: 2, y: 2, z: 4, core: 2. Of those that a mesh axis runs over, the one named last changes fastest.
Arguments:
- hidden_in: bfloat16 [4608, 896], P(('dp', 'col'), 'row'), may hold values from -6 to 6
- norm1_gain: float32 [896], P('row'), may hold values from 0.5 to 1.5
- qkv_weight: bfloat16 [896, 1152], P('row', 'col'), may hold values from -0.1875 to 0.1875
- qkv_bias: bfloat16 [1152], P('col'), may hold values from -3 to 3
- out_weight: bfloat16 [896, 896], P('col', 'row'), may hold values from -0.5 to 0.5
- norm2_gain: float32 [896], P('row'), may hold values from 0.5 to 1.5
- gate_weight: bfloat16 [896, 4864], P('row', 'col'), may hold values from -0.1875 to 0.1875
- up_weight: bfloat16 [896, 4864], P('row', 'col'), may hold values from -0.1875 to 0.1875
- down_weight: bfloat16 [4864, 896], P('col', 'row'), may hold values from -0.125 to 0.125
- seq_lens: int32 [2, 9], P('dp'), may hold values from 1 to 1024, 2304 in all within a row
- out_grad: bfloat16 [4608, 896], P(('dp', 'col'), 'row'), may hold values from -6 to 6
Outputs:
- hidden_out: bfloat16 [4608, 896], P(('dp', 'col'), 'row')
- hidden_grad: float32 [4608, 896], P(('dp', 'col'), 'row')
- norm1_gain_grad: float32 [896], P('row')
- qkv_weight_grad: float32 [896, 1152], P('row', 'col')
- qkv_bias_grad: float32 [1152], P('col')
- out_weight_grad: float32 [896, 896], P('col', 'row')
- norm2_gain_grad: float32 [896], P('row')
- gate_weight_grad: float32 [896, 4864], P('row', 'col')
- up_weight_grad: float32 [896, 4864], P('row', 'col')
- down_weight_grad: float32 [4864, 896], P('col', 'row')
Inputs may be any that keep to these rules, and one draw needn't show every extreme that they name: Row i of seq_lens lists in order the lengths of the 9 sequences packed into group i; each row sums to 2304 and its longest is 1024.
All inputs are finite; a program needn't handle non-finite values.
Results may differ from a plain program's by a relative error of at most 0.014.
Values may be sent and summed in bfloat16 or wider, within the bound.
No kernel may reach another device: no remote copies, remote signals or barrier semaphores. Data moves between devices by JAX's collectives and lax.ppermute only.
A program may use at most 128 MiB of HBM per device.

v0:
```python
import jax
import jax.numpy as jnp
from jax import lax
from jax.sharding import PartitionSpec as P

D = 896
HEADS = 14
KV_HEADS = 2
HEAD_DIM = 64
REACH = 8


norm_eps = 1e-06
rope_base = 1000000.0
masked_score = -1e30


def shifted(array, axis, by):
    count = lax.axis_size(axis)
    pairs = [(i, i + by) for i in range(count) if 0 <= i + by < count]
    return lax.ppermute(array, axis, pairs)


def feature_total(values):
    return lax.psum(values, "row")


def gather_cols(values):
    return lax.all_gather(values, "col", axis=0, tiled=True)


def gather_rows(values):
    return lax.all_gather(values, "row", axis=0, tiled=True)


def spread_heads(values):
    return lax.all_to_all(values, "col", split_axis=0, concat_axis=1, tiled=True)


def collect_heads(values):
    return lax.all_to_all(values, "col", split_axis=1, concat_axis=0, tiled=True)


def product(left, right, flipped):
    if flipped:
        return lax.dot_general(
            left, right, (((1,), (1,)), ((), ())), preferred_element_type=jnp.float32
        )
    return jnp.dot(left, right, preferred_element_type=jnp.float32)


def contract_rows(left, right):
    return lax.dot_general(
        left, right, (((0,), (0,)), ((), ())), preferred_element_type=jnp.float32
    )


def sum_over_rows(whole, weight, flipped):
    mine = whole.shape[0] // lax.axis_size("row")

    def partial_term(start, count):
        return product(whole, weight, flipped)

    return lax.psum_scatter(
        partial_term(jnp.int32(0), mine * lax.axis_size("row")),
        "row",
        scatter_dimension=0,
        tiled=True,
    )


def sum_over_cols(whole, weight, flipped):
    mine = whole.shape[0] // lax.axis_size("col")

    def partial_term(start, count):
        return product(whole, weight, flipped)

    return lax.psum_scatter(
        partial_term(jnp.int32(0), mine * lax.axis_size("col")),
        "col",
        scatter_dimension=0,
        tiled=True,
    )


def locate(indices, lengths):
    ends = jnp.cumsum(lengths)
    starts = ends - lengths
    segment = jnp.sum((indices[:, None] >= ends[None, :]).astype(jnp.int32), 1)
    chosen = segment[:, None] == jnp.arange(lengths.shape[0], dtype=jnp.int32)[None, :]
    position = indices - jnp.sum(jnp.where(chosen, starts[None, :], 0), 1)
    return (segment, position)


def rope_tables(position):
    half = HEAD_DIM // 2
    rates = rope_base ** (-(jnp.arange(half, dtype=jnp.float32) * 2.0) / HEAD_DIM)
    angles = position.astype(jnp.float32)[:, None] * rates[None, :]
    cosine = jnp.cos(angles)
    sine = jnp.sin(angles)
    return (jnp.concatenate([cosine, cosine], -1), jnp.concatenate([sine, sine], -1))


def rotate(values, cosine, sine):
    half = values.shape[-1] // 2
    turned = jnp.concatenate([-values[..., half:], values[..., :half]], -1)
    return values * cosine[:, None, :] + turned * sine[:, None, :]


def rotate_back(grads, cosine, sine):
    half = grads.shape[-1] // 2
    moved = grads * sine[:, None, :]
    turned = jnp.concatenate([moved[..., half:], -moved[..., :half]], -1)
    return grads * cosine[:, None, :] + turned


def score_block(group_queries, group_keys, allowed, scale):
    scores = (
        jnp.einsum("qha,ka->hqk", group_queries, group_keys, preferred_element_type=jnp.float32)
        * scale
    )
    return jnp.where(allowed[None], scores, masked_score)


def body(
    hidden_in,
    norm1_gain,
    qkv_weight,
    qkv_bias,
    out_weight,
    norm2_gain,
    gate_weight,
    up_weight,
    down_weight,
    seq_lens,
    out_grad,
):
    row_count = lax.axis_size("row")
    col_count = lax.axis_size("col")
    row_place = lax.axis_index("row")
    col_place = lax.axis_index("col")
    quarter = hidden_in.shape[0]
    block_rows = quarter // row_count
    lengths = seq_lens[0]
    group_heads = HEADS // KV_HEADS
    scale = HEAD_DIM ** (-0.5)
    query_width = HEADS * HEAD_DIM
    kv_width = KV_HEADS * HEAD_DIM
    ff_cols = gate_weight.shape[1]
    inputs = hidden_in.astype(jnp.float32)
    scale1 = lax.rsqrt(feature_total(jnp.sum(inputs * inputs, 1)) / D + norm_eps)
    normed1 = (inputs * scale1[:, None] * norm1_gain).astype(jnp.bfloat16)
    normed1_all = gather_cols(normed1)
    projected = sum_over_rows(normed1_all, qkv_weight, False) + qkv_bias.astype(jnp.float32)
    projected = spread_heads(projected)
    first = (row_place * col_count + col_place) * block_rows
    query_index = first + jnp.arange(block_rows, dtype=jnp.int32)
    query_segment, query_position = locate(query_index, lengths)
    cosine, sine = rope_tables(query_position)
    queries = rotate(
        projected[:, :query_width].reshape(block_rows, HEADS, HEAD_DIM), cosine, sine
    ).astype(jnp.bfloat16)
    keys = rotate(
        projected[:, query_width : query_width + kv_width].reshape(block_rows, KV_HEADS, HEAD_DIM),
        cosine,
        sine,
    )
    values = projected[:, query_width + kv_width :]
    own_pair = jnp.concatenate([keys.reshape(block_rows, kv_width), values], 1).astype(jnp.bfloat16)
    pieces = []
    for hop in range(REACH, 0, -1):
        pieces.append(shifted(own_pair, ("row", "col"), hop))
    pieces.append(own_pair)
    window = jnp.concatenate(pieces, 0)
    key_index = first - REACH * block_rows + jnp.arange((REACH + 1) * block_rows, dtype=jnp.int32)
    key_segment = locate(key_index, lengths)[0]
    allowed = (
        (key_index[None, :] >= 0)
        & (key_segment[None, :] == query_segment[:, None])
        & (key_index[None, :] <= query_index[:, None])
    )
    attended_parts = []
    log_totals = []
    for group in range(KV_HEADS):
        group_queries = queries[:, group * group_heads : (group + 1) * group_heads]
        group_keys = window[:, group * HEAD_DIM : (group + 1) * HEAD_DIM]
        group_values = window[:, kv_width + group * HEAD_DIM : kv_width + (group + 1) * HEAD_DIM]
        scores = score_block(group_queries, group_keys, allowed, scale)
        top = jnp.max(scores, -1, keepdims=True)
        raised = jnp.exp(scores - top)
        total = jnp.sum(raised, -1, keepdims=True)
        weights = (raised / total).astype(jnp.bfloat16)
        attended_parts.append(
            jnp.einsum("hqk,ka->qha", weights, group_values, preferred_element_type=jnp.float32)
        )
        log_totals.append(top + jnp.log(total))
    attended = (
        jnp.concatenate(attended_parts, 1).reshape(block_rows, query_width).astype(jnp.bfloat16)
    )
    attended_all = gather_rows(collect_heads(attended))
    middle = inputs + sum_over_cols(attended_all, out_weight, False)
    scale2 = lax.rsqrt(feature_total(jnp.sum(middle * middle, 1)) / D + norm_eps)
    normed2 = (middle * scale2[:, None] * norm2_gain).astype(jnp.bfloat16)
    normed2_all = gather_cols(normed2)
    upstream_all = gather_cols(out_grad)
    paired_weight = jnp.concatenate([gate_weight, up_weight], 1)
    paired = sum_over_rows(normed2_all, paired_weight, False)
    gate = paired[:, :ff_cols]
    up = paired[:, ff_cols:]
    sigma = jax.nn.sigmoid(gate)
    hidden = (gate * sigma * up).astype(jnp.bfloat16)
    hidden_all = gather_rows(hidden)
    hidden_out = (middle + sum_over_cols(hidden_all, down_weight, False)).astype(jnp.bfloat16)
    upstream = out_grad.astype(jnp.float32)
    down_grad = contract_rows(hidden_all, upstream_all)
    grad_hidden = sum_over_rows(upstream_all, down_weight, True)
    grad_gate = grad_hidden * up * sigma * (1.0 + gate * (1.0 - sigma))
    grad_up = grad_hidden * gate * sigma
    grad_paired_all = gather_rows(jnp.concatenate([grad_gate, grad_up], 1).astype(jnp.bfloat16))
    paired_grad = contract_rows(normed2_all, grad_paired_all)
    gate_grad = paired_grad[:, :ff_cols]
    up_grad = paired_grad[:, ff_cols:]
    grad_normed2 = sum_over_cols(grad_paired_all, paired_weight, True)
    gain2_grad = jnp.sum(grad_normed2 * middle * scale2[:, None], 0)
    scaled2 = grad_normed2 * norm2_gain
    middle_sum = feature_total(jnp.sum(scaled2 * middle, 1))
    grad_middle = (
        upstream + scale2[:, None] * scaled2 - middle * (scale2**3 * middle_sum / D)[:, None]
    )
    middle_all = gather_cols(grad_middle.astype(jnp.bfloat16))
    out_w_grad = contract_rows(attended_all, middle_all)
    grad_attended = spread_heads(sum_over_rows(middle_all, out_weight, True)).astype(jnp.bfloat16)
    grad_heads = grad_attended.reshape(block_rows, HEADS, HEAD_DIM)
    query_grads = []
    key_grads = []
    value_grads = []
    for group in range(KV_HEADS):
        group_queries = queries[:, group * group_heads : (group + 1) * group_heads]
        group_keys = window[:, group * HEAD_DIM : (group + 1) * HEAD_DIM]
        group_values = window[:, kv_width + group * HEAD_DIM : kv_width + (group + 1) * HEAD_DIM]
        group_grads = grad_heads[:, group * group_heads : (group + 1) * group_heads]
        scores = score_block(group_queries, group_keys, allowed, scale)
        probs = jnp.exp(scores - log_totals[group])
        grad_probs = jnp.einsum(
            "qha,ka->hqk", group_grads, group_values, preferred_element_type=jnp.float32
        )
        grad_scores = (
            probs * (grad_probs - jnp.sum(probs * grad_probs, -1, keepdims=True))
        ).astype(jnp.bfloat16)
        query_grads.append(
            jnp.einsum("hqk,ka->qha", grad_scores, group_keys, preferred_element_type=jnp.float32)
            * scale
        )
        key_grads.append(
            jnp.einsum(
                "hqk,qha->ka", grad_scores, group_queries, preferred_element_type=jnp.float32
            )
            * scale
        )
        value_grads.append(
            jnp.einsum(
                "hqk,qha->ka",
                probs.astype(jnp.bfloat16),
                group_grads,
                preferred_element_type=jnp.float32,
            )
        )
    grad_window = jnp.concatenate(key_grads + value_grads, 1)
    grad_pair = grad_window[REACH * block_rows :]
    for hop in range(1, REACH + 1):
        piece = grad_window[(REACH - hop) * block_rows : (REACH - hop + 1) * block_rows]
        grad_pair = grad_pair + shifted(piece.astype(jnp.bfloat16), ("row", "col"), -hop).astype(
            piece.dtype
        )
    grad_queries = rotate_back(jnp.concatenate(query_grads, 1), cosine, sine)
    grad_keys = rotate_back(
        grad_pair[:, :kv_width].reshape(block_rows, KV_HEADS, HEAD_DIM), cosine, sine
    )
    grad_projected = jnp.concatenate(
        [
            grad_queries.reshape(block_rows, query_width),
            grad_keys.reshape(block_rows, kv_width),
            grad_pair[:, kv_width:],
        ],
        1,
    ).astype(jnp.bfloat16)
    projected_all = gather_rows(collect_heads(grad_projected))
    qkv_grad = contract_rows(normed1_all, projected_all)
    bias_grad = jnp.sum(projected_all, 0, dtype=jnp.float32)
    grad_normed1 = sum_over_cols(projected_all, qkv_weight, True)
    gain1_grad = jnp.sum(grad_normed1 * inputs * scale1[:, None], 0)
    scaled1 = grad_normed1 * norm1_gain
    input_sum = feature_total(jnp.sum(scaled1 * inputs, 1))
    hidden_grad = (
        grad_middle + scale1[:, None] * scaled1 - inputs * (scale1**3 * input_sum / D)[:, None]
    )
    qkv_grad, bias_grad, out_w_grad, gate_grad, up_grad, down_grad = (
        lax.psum(qkv_grad.astype(jnp.bfloat16), "dp").astype(jnp.float32),
        lax.psum(bias_grad.astype(jnp.bfloat16), "dp").astype(jnp.float32),
        lax.psum(out_w_grad.astype(jnp.bfloat16), "dp").astype(jnp.float32),
        lax.psum(gate_grad.astype(jnp.bfloat16), "dp").astype(jnp.float32),
        lax.psum(up_grad.astype(jnp.bfloat16), "dp").astype(jnp.float32),
        lax.psum(down_grad.astype(jnp.bfloat16), "dp").astype(jnp.float32),
    )
    gain1_grad, gain2_grad = lax.psum((gain1_grad, gain2_grad), ("dp", "col"))
    return (
        hidden_out,
        hidden_grad,
        gain1_grad,
        qkv_grad,
        bias_grad,
        out_w_grad,
        gain2_grad,
        gate_grad,
        up_grad,
        down_grad,
    )


def solution(mesh):
    return jax.shard_map(
        body,
        mesh=mesh,
        in_specs=(
            P(("dp", "col"), "row"),
            P("row"),
            P("row", "col"),
            P("col"),
            P("col", "row"),
            P("row"),
            P("row", "col"),
            P("row", "col"),
            P("col", "row"),
            P("dp", None),
            P(("dp", "col"), "row"),
        ),
        out_specs=(
            P(("dp", "col"), "row"),
            P(("dp", "col"), "row"),
            P("row"),
            P("row", "col"),
            P("col"),
            P("col", "row"),
            P("row"),
            P("row", "col"),
            P("row", "col"),
            P("col", "row"),
        ),
        check_vma=False,
    )
```

profile of v0, /device:TPU:0, one launch (start us, length us, event | category | flops | bytes accessed | tf_op | source)
XLA Modules:
  0.0 1043.9 jit_solution(15409394211066509958)
XLA Ops:
  8.3 8.3 psum.84
  18.9 24.0 %all-gather = bf16[4,576,224]{1,2,0:T(8,128)(2,1)S(1)} all-gather(bf16[1,576,224]{1,2,0:T(8,128)(2,1)S(1)} %fusion.46), channel_id=1, replica_groups=mesh['dp'=2,'row'=4,'col'=4] {'col'}, dimensions={0}, use_global_device_ids=true | all-gather | bytes 1290240 | tf_op jit(solution)/shard_map/all_gather | solution.py:29
  50.4 39.0 %reduce-scatter.25.cloned.1.call-done = f32[576,288]{1,0:T(8,128)} async-done(((f32[2304,288]{1,0:T(8,128)}), f32[576,288]{1,0:T(8,128)}) %reduce-scatter.25.cloned.1.call-update) | async-done | bytes 663568 | tf_op jit(solution)/shard_map/reduce_scatter | solution.py:64
  96.7 21.6 %all-to-all-done = f32[4,144,288]{2,1,0:T(8,128)S(1)} async-done(((f32[4,144,288]{2,1,0:T(8,128)}), f32[4,144,288]{2,1,0:T(8,128)S(1)}, u32[]{:S(2)}, u32[]{:S(2)}) %all-to-all-start) | async-done | bytes 663584 | tf_op jit(solution)/shard_map/all_to_all | solution.py:37
  151.9 18.2 %all_to_all.64 = bf16[144,4,224]{2,0,1:T(8,128)(2,1)S(1)} all-to-all(bf16[144,4,224]{2,0,1:T(8,128)(2,1)S(1)} %copy.80), channel_id=1, replica_groups=mesh['dp'=2,'row'=4,'col'=4] {'col'}, dimensions={1} | all-to-all | bytes 516096 | tf_op jit(solution)/shard_map/all_to_all | solution.py:41
  170.3 9.0 all-gather.1
  185.0 39.2 %all-gather.3 = bf16[4,576,224]{1,2,0:T(8,128)(2,1)S(1)} all-gather(bf16[1,576,224]{1,2,0:T(8,128)(2,1)S(1)} %bitcast.177), channel_id=1, replica_groups=mesh['dp'=2,'row'=4,'col'=4] {'col'}, dimensions={0}, use_global_device_ids=true | all-gather | bytes 1290240 | tf_op jit(solution)/shard_map/all_gather | solution.py:29
  227.9 6.1 fusion.80
  234.0 12.9 %reduce-scatter.27.cloned.1.call-done = f32[576,224]{1,0:T(8,128)} async-done(((f32[2304,224]{1,0:T(8,128)}), f32[576,224]{1,0:T(8,128)}) %reduce-scatter.27.cloned.1.call-update) | async-done | bytes 516112
  248.3 7.5 psum.85
  255.9 23.3 %all-gather.2 = bf16[4,576,224]{1,2,0:T(8,128)(2,1)S(1)} all-gather(bf16[1,576,224]{1,2,0:T(8,128)(2,1)S(1)} %fusion.45), channel_id=1, replica_groups=mesh['dp'=2,'row'=4,'col'=4] {'col'}, dimensions={0}, use_global_device_ids=true | all-gather | bytes 1290240 | tf_op jit(solution)/shard_map/all_gather | solution.py:29
  282.9 11.2 %fusion.37 = f32[2304,2432]{1,0:T(8,128)} fusion(bf16[2304,224]{0,1:T(8,128)(2,1)S(1)} %reshape.213, bf16[224,1216]{1,0:T(8,128)(2,1)} %param.18, bf16[224,1216]{1,0:T(8,128)(2,1)} %param.17), kind=kOutput, calls=%fused_computation.68 | convolution fusion | flops 2512470016 | bytes 24535040 | tf_op jit(solution)/shard_map/dot_general | solution.py:49
  294.2 50.6 %reduce-scatter.23.cloned.1.call-done = f32[576,1216]{1,0:T(8,128)} async-done(((f32[2304,1216]{1,0:T(8,128)}), f32[576,1216]{1,0:T(8,128)}) %reduce-scatter.23.cloned.1.call-update) | async-done | bytes 2801680 | tf_op jit(solution)/shard_map/reduce_scatter | solution.py:64
  344.8 165.2 %reduce-scatter.21.cloned.1.call-done = f32[576,2432]{1,0:T(8,128)} async-done(((f32[2304,2432]{1,0:T(8,128)}), f32[576,2432]{1,0:T(8,128)}) %reduce-scatter.21.cloned.1.call-update) | async-done | bytes 5603344 | tf_op jit(solution)/shard_map/reduce_scatter | solution.py:64
  510.0 5.3 multiply_convert_fusion.1
  517.8 74.4 %all-gather.12.cloned.1.call-done = bf16[2304,2432]{1,0:T(8,128)(2,1)} async-done(((bf16[576,2432]{1,0:T(8,128)(2,1)}), bf16[2304,2432]{1,0:T(8,128)(2,1)}) %all-gather.12.cloned.1.call-update) | async-done | bytes 11206672 | tf_op jit(solution)/shard_map/all_gather | solution.py:33
  592.2 9.3 fusion.36
  601.8 47.9 %reduce-scatter.31.cloned.1.call-done = f32[576,224]{1,0:T(8,128)} async-done(((f32[2304,224]{1,0:T(8,128)}), f32[576,224]{1,0:T(8,128)}) %reduce-scatter.31.cloned.1.call-update) | async-done | bytes 516112
  651.7 6.4 psum.86
  658.3 22.5 %all-gather.4 = bf16[4,576,224]{1,2,0:T(8,128)(2,1)S(1)} all-gather(bf16[1,576,224]{1,2,0:T(8,128)(2,1)S(1)} %convert_bitcast_fusion.1), channel_id=1, replica_groups=mesh['dp'=2,'row'=4,'col'=4] {'col'}, dimensions={0}, use_global_device_ids=true | all-gather | bytes 1290240 | tf_op jit(solution)/shard_map/all_gather | solution.py:29
  687.6 32.7 %reduce-scatter.33.cloned.1.call-done = f32[576,224]{1,0:T(8,128)} async-done(((f32[2304,224]{1,0:T(8,128)}), f32[576,224]{1,0:T(8,128)}) %reduce-scatter.33.cloned.1.call-update) | async-done | bytes 516112 | tf_op jit(solution)/shard_map/reduce_scatter | solution.py:64
  725.6 15.2 %all-to-all-done.2 = f32[4,144,224]{2,1,0:T(8,128)} async-done(((f32[4,144,224]{2,1,0:T(8,128)}), f32[4,144,224]{2,1,0:T(8,128)}, u32[]{:S(2)}, u32[]{:S(2)}) %all-to-all-start.2) | async-done | bytes 516128 | tf_op jit(solution)/shard_map/all_to_all | solution.py:37
  795.5 15.8 %all_to_all.65 = bf16[144,4,288]{2,0,1:T(8,128)(2,1)} all-to-all(bf16[144,4,288]{2,0,1:T(8,128)(2,1)S(1)} %copy.91), channel_id=1, replica_groups=mesh['dp'=2,'row'=4,'col'=4] {'col'}, dimensions={1} | all-to-all | bytes 663552 | tf_op jit(solution)/shard_map/all_to_all | solution.py:41
  813.3 5.8 fusion.79
  819.2 5.4 convolution_convert_fusion.1
  824.6 7.4 convolution_convert_fusion
  834.3 5.8 all-gather.14.cloned.1.call-done
  853.7 36.8 %reduce-scatter.29.cloned.1.call-done = f32[576,224]{1,0:T(8,128)} async-done(((f32[2304,224]{1,0:T(8,128)}), f32[576,224]{1,0:T(8,128)}) %reduce-scatter.29.cloned.1.call-update) | async-done | bytes 516112
  899.8 55.3 %all-reduce.4.cloned.1.call-done = (bf16[224,288]{0,1:T(8,128)(2,1)}, bf16[224,224]{1,0:T(8,128)(2,1)}, bf16[224,1216]{1,0:T(8,128)(2,1)}, bf16[224,1216]{1,0:T(8,128)(2,1)}, bf16[1216,224]{0,1:T(8,128)(2,1)}) async-done(((bf16[224,288]{0,1:T(8,128)(2,1)}, bf16[224,224]{1,0:T(8,128)(2,1)}, bf16[224,1216]{1,0:T(8,128)(2,1)}, bf16[224,1216]{1,0:T(8,128)(2,1)}, bf16[1216,224]{0,1:T(8,128)(2,1)}), ...) | async-done | bytes 1863696 | tf_op jit(solution)/shard_map/psum | solution.py:298
  962.1 43.2 %reduce-scatter.35.cloned.1.call-done = f32[576,224]{1,0:T(8,128)} async-done(((f32[2304,224]{1,0:T(8,128)}), f32[576,224]{1,0:T(8,128)}) %reduce-scatter.35.cloned.1.call-update) | async-done | bytes 516112
  1006.9 6.4 psum.87
  1013.3 20.9 %all-reduce = (f32[224]{0:T(256)}, f32[224]{0:T(256)}) all-reduce(f32[224]{0:T(256)S(1)} %get-tuple-element.12, f32[224]{0:T(256)S(1)} %copy-done.46), channel_id=1, replica_groups=mesh['dp'=2,'row'=4,'col'=4] {'dp','col'}, use_global_device_ids=true, to_apply=%region_27.28 | all-reduce | flops 448 | bytes 3584 | tf_op jit(solution)/shard_map/psum | solution.py:305
  (281 shorter events, 175.4 us)
Async XLA Ops:
  7.2 220.7 %copy-start = (bf16[1216,224]{0,1:T(8,128)(2,1)S(1)}, bf16[1216,224]{0,1:T(8,128)(2,1)}, u32[]{:S(2)}) copy-start(bf16[1216,224]{0,1:T(8,128)(2,1)} %param.19) | copy-start | bytes 1634308
  7.2 82.2 %reduce-scatter.25.cloned.1.call-start = ((), (), s32[]{:S(2)}) async-start(), calls=%async_computation.17 | async-start | bytes 4423680 | tf_op jit(solution)/shard_map/reduce_scatter | solution.py:64
  91.5 26.8 %all-to-all-start = ((f32[4,144,288]{2,1,0:T(8,128)}), f32[4,144,288]{2,1,0:T(8,128)S(1)}, u32[]{:S(2)}, u32[]{:S(2)}) async-start(f32[4,144,288]{2,1,0:T(8,128)} %bitcast.1), calls=%async_computation | async-start | bytes 1769472 | tf_op jit(solution)/shard_map/all_to_all | solution.py:37
  96.1 150.8 %reduce-scatter.27.cloned.1.call-start = ((), (), s32[]{:S(2)}) async-start(), calls=%async_computation.18 | async-start | bytes 2949120
  118.9 10.8 %collective-permute-start = (bf16[144,256]{0,1:T(8,128)(2,1)S(1)}, bf16[144,256]{0,1:T(8,128)(2,1)S(1)}, u32[]{:S(2)}, u32[]{:S(2)}) collective-permute-start(bf16[144,256]{0,1:T(8,128)(2,1)S(1)} %pad_maximum_fusion.8), channel_id=1, source_target_pairs={{0,8},{1,9},{2,10},{3,11},{4,12},{5,13},{6,14},{7,15},{16,24},{17,... | collective-permute-start | bytes 221192 | tf_op jit(solution)/shard_map/ppermute | solution.py:21
  121.4 13.0 %collective-permute-start.1 = (bf16[144,256]{0,1:T(8,128)(2,1)S(1)}, bf16[144,256]{0,1:T(8,128)(2,1)S(1)}, u32[]{:S(2)}, u32[]{:S(2)}) collective-permute-start(bf16[144,256]{0,1:T(8,128)(2,1)S(1)} %pad_maximum_fusion.8), channel_id=1, source_target_pairs={{0,7},{1,8},{2,9},{3,10},{4,11},{5,12},{6,13},{7,14},{8,15},{16,23... | collective-permute-start | bytes 221192 | tf_op jit(solution)/shard_map/ppermute | solution.py:21
  122.7 13.0 %collective-permute-start.2 = (bf16[144,256]{0,1:T(8,128)(2,1)S(1)}, bf16[144,256]{0,1:T(8,128)(2,1)S(1)}, u32[]{:S(2)}, u32[]{:S(2)}) collective-permute-start(bf16[144,256]{0,1:T(8,128)(2,1)S(1)} %pad_maximum_fusion.8), channel_id=1, source_target_pairs={{0,6},{1,7},{2,8},{3,9},{4,10},{5,11},{6,12},{7,13},{8,14},{9,15},... | collective-permute-start | bytes 221192 | tf_op jit(solution)/shard_map/ppermute | solution.py:21
  124.0 16.9 %collective-permute-start.3 = (bf16[144,256]{0,1:T(8,128)(2,1)S(1)}, bf16[144,256]{0,1:T(8,128)(2,1)S(1)}, u32[]{:S(2)}, u32[]{:S(2)}) collective-permute-start(bf16[144,256]{0,1:T(8,128)(2,1)S(1)} %pad_maximum_fusion.8), channel_id=1, source_target_pairs={{0,5},{1,6},{2,7},{3,8},{4,9},{5,10},{6,11},{7,12},{8,13},{9,14},{... | collective-permute-start | bytes 221192 | tf_op jit(solution)/shard_map/ppermute | solution.py:21
  127.1 13.9 %collective-permute-start.4 = (bf16[144,256]{0,1:T(8,128)(2,1)S(1)}, bf16[144,256]{0,1:T(8,128)(2,1)S(1)}, u32[]{:S(2)}, u32[]{:S(2)}) collective-permute-start(bf16[144,256]{0,1:T(8,128)(2,1)S(1)} %pad_maximum_fusion.8), channel_id=1, source_target_pairs={{0,4},{1,5},{2,6},{3,7},{4,8},{5,9},{6,10},{7,11},{8,12},{9,13},{1... | collective-permute-start | bytes 221192 | tf_op jit(solution)/shard_map/ppermute | solution.py:21
  129.7 11.2 %collective-permute-start.5 = (bf16[144,256]{0,1:T(8,128)(2,1)S(1)}, bf16[144,256]{0,1:T(8,128)(2,1)S(1)}, u32[]{:S(2)}, u32[]{:S(2)}) collective-permute-start(bf16[144,256]{0,1:T(8,128)(2,1)S(1)} %pad_maximum_fusion.8), channel_id=1, source_target_pairs={{0,3},{1,4},{2,5},{3,6},{4,7},{5,8},{6,9},{7,10},{8,11},{9,12},{10... | collective-permute-start | bytes 221192 | tf_op jit(solution)/shard_map/ppermute | solution.py:21
  134.4 6.6 collective-permute-start.6
  135.7 6.7 collective-permute-start.7
  185.0 159.8 %reduce-scatter.23.cloned.1.call-start = ((), (), s32[]{:S(2)}) async-start(), calls=%async_computation.14 | async-start | bytes 14745600 | tf_op jit(solution)/shard_map/reduce_scatter | solution.py:64
  234.0 276.0 %reduce-scatter.21.cloned.1.call-start = ((), (), s32[]{:S(2)}) async-start(), calls=%async_computation.12 | async-start | bytes 28016640 | tf_op jit(solution)/shard_map/reduce_scatter | solution.py:64
  294.1 298.1 %all-gather.12.cloned.1.call-start = ((), (), s32[]{:S(2)}) async-start(), calls=%async_computation.15 | async-start | bytes 14008320 | tf_op jit(solution)/shard_map/all_gather | solution.py:33
  517.7 131.9 %reduce-scatter.31.cloned.1.call-start = ((), (), s32[]{:S(2)}) async-start(), calls=%async_computation.20 | async-start | bytes 2949120
  601.5 118.7 %reduce-scatter.33.cloned.1.call-start = ((), (), s32[]{:S(2)}) async-start(), calls=%async_computation.21 | async-start | bytes 2949120 | tf_op jit(solution)/shard_map/reduce_scatter | solution.py:64
  720.2 20.6 %all-to-all-start.2 = ((f32[4,144,224]{2,1,0:T(8,128)}), f32[4,144,224]{2,1,0:T(8,128)}, u32[]{:S(2)}, u32[]{:S(2)}) async-start(f32[4,144,224]{2,1,0:T(8,128)} %bitcast.182), calls=%async_computation.4 | async-start | bytes 1179648 | tf_op jit(solution)/shard_map/all_to_all | solution.py:37
  724.8 88.5 %all-gather.10.cloned.1.call-start = ((), (), s32[]{:S(2)}) async-start(), calls=%async_computation.13 | async-start | bytes 7372800 | tf_op jit(solution)/shard_map/all_gather | solution.py:33
  725.5 114.6 %all-gather.14.cloned.1.call-start = ((), (), s32[]{:S(2)}) async-start(), calls=%async_computation.16 | async-start | bytes 1843200 | tf_op jit(solution)/shard_map/all_gather | solution.py:33
  758.8 10.6 %collective-permute-start.10 = (bf16[144,256]{0,1:T(8,128)(2,1)S(1)}, bf16[144,256]{0,1:T(8,128)(2,1)S(1)}, u32[]{:S(2)}, u32[]{:S(2)}) collective-permute-start(bf16[144,256]{0,1:T(8,128)(2,1)S(1)} %get-tuple-element.38), channel_id=1, source_target_pairs={{3,0},{4,1},{5,2},{6,3},{7,4},{8,5},{9,6},{10,7},{11,8},{12,9},{13... | collective-permute-start | bytes 221192 | tf_op jit(solution)/shard_map/ppermute | solution.py:21
  760.0 10.6 %collective-permute-start.11 = (bf16[144,256]{0,1:T(8,128)(2,1)S(1)}, bf16[144,256]{0,1:T(8,128)(2,1)S(1)}, u32[]{:S(2)}, u32[]{:S(2)}) collective-permute-start(bf16[144,256]{0,1:T(8,128)(2,1)S(1)} %get-tuple-element.37), channel_id=1, source_target_pairs={{4,0},{5,1},{6,2},{7,3},{8,4},{9,5},{10,6},{11,7},{12,8},{13,9},{1... | collective-permute-start | bytes 221192 | tf_op jit(solution)/shard_map/ppermute | solution.py:21
  761.4 10.6 %collective-permute-start.12 = (bf16[144,256]{0,1:T(8,128)(2,1)S(1)}, bf16[144,256]{0,1:T(8,128)(2,1)S(1)}, u32[]{:S(2)}, u32[]{:S(2)}) collective-permute-start(bf16[144,256]{0,1:T(8,128)(2,1)S(1)} %get-tuple-element.36), channel_id=1, source_target_pairs={{5,0},{6,1},{7,2},{8,3},{9,4},{10,5},{11,6},{12,7},{13,8},{14,9},{... | collective-permute-start | bytes 221192 | tf_op jit(solution)/shard_map/ppermute | solution.py:21
  766.5 9.7 collective-permute-start.13
  767.8 11.5 %collective-permute-start.14 = (bf16[144,256]{0,1:T(8,128)(2,1)}, bf16[144,256]{0,1:T(8,128)(2,1)}, u32[]{:S(2)}, u32[]{:S(2)}) collective-permute-start(bf16[144,256]{0,1:T(8,128)(2,1)} %get-tuple-element.34), channel_id=1, source_target_pairs={{7,0},{8,1},{9,2},{10,3},{11,4},{12,5},{13,6},{14,7},{15,8},{23,16... | collective-permute-start | bytes 221192 | tf_op jit(solution)/shard_map/ppermute | solution.py:21
  769.3 13.8 %collective-permute-start.15 = (bf16[144,256]{0,1:T(8,128)(2,1)}, bf16[144,256]{0,1:T(8,128)(2,1)}, u32[]{:S(2)}, u32[]{:S(2)}) collective-permute-start(bf16[144,256]{0,1:T(8,128)(2,1)} %get-tuple-element.33), channel_id=1, source_target_pairs={{8,0},{9,1},{10,2},{11,3},{12,4},{13,5},{14,6},{15,7},{24,16},{25,... | collective-permute-start | bytes 221192 | tf_op jit(solution)/shard_map/ppermute | solution.py:21
  770.7 12.5 %collective-permute-start.8 = (bf16[144,256]{0,1:T(8,128)(2,1)}, bf16[144,256]{0,1:T(8,128)(2,1)}, u32[]{:S(2)}, u32[]{:S(2)}) collective-permute-start(bf16[144,256]{0,1:T(8,128)(2,1)} %get-tuple-element.32), channel_id=1, source_target_pairs={{1,0},{2,1},{3,2},{4,3},{5,4},{6,5},{7,6},{8,7},{9,8},{10,9},{11,1... | collective-permute-start | bytes 221192 | tf_op jit(solution)/shard_map/ppermute | solution.py:21
  772.0 11.5 %collective-permute-start.9 = (bf16[144,256]{0,1:T(8,128)(2,1)}, bf16[144,256]{0,1:T(8,128)(2,1)}, u32[]{:S(2)}, u32[]{:S(2)}) collective-permute-start(bf16[144,256]{0,1:T(8,128)(2,1)} %get-tuple-element.39), channel_id=1, source_target_pairs={{2,0},{3,1},{4,2},{5,3},{6,4},{7,5},{8,6},{9,7},{10,8},{11,9},{12,... | collective-permute-start | bytes 221192 | tf_op jit(solution)/shard_map/ppermute | solution.py:21
  813.3 77.2 %reduce-scatter.29.cloned.1.call-start = ((), (), s32[]{:S(2)}) async-start(), calls=%async_computation.19 | async-start | bytes 2949120
  819.2 135.9 %all-reduce.4.cloned.1.call-start = ((), (), s32[]{:S(2)}) async-start(), calls=%async_computation.23 | async-start | bytes 3964928 | tf_op jit(solution)/shard_map/psum | solution.py:298
  850.1 155.3 %reduce-scatter.35.cloned.1.call-start = ((), (), s32[]{:S(2)}) async-start(), calls=%async_computation.22 | async-start | bytes 2949120
  957.3 76.9 %copy-start.4 = (f32[576,224]{0,1:T(8,128)S(1)}, f32[576,224]{0,1:T(8,128)}, u32[]{:S(2)}) copy-start(f32[576,224]{0,1:T(8,128)} %copy-done.3) | copy-start | bytes 1548292
  (51 other events, 810.5 us)
Sparse Core Ops, SparseCore 0:
  49.4 39.9 reduce-scatter.24
  185.1 61.7 reduce-scatter.26
  249.7 95.0 reduce-scatter.22
  347.5 162.4 reduce-scatter.20
  517.9 74.2 all-gather.11
  601.6 48.0 reduce-scatter.30
  687.7 32.4 reduce-scatter.32
  727.3 47.4 all-gather.9
  813.4 26.7 all-gather.13
  842.4 48.0 reduce-scatter.28
  894.4 60.6 all-reduce.3
  957.3 48.0 reduce-scatter.34
where the time goes:
time: 1050 us; the launch traced here: 1040 us
  waiting for transfers between devices  609 us (58%)
  blocking collectives  207 us (20%)
  matrix products  77.6 us (7%)
  local copies, waits for them, and re-layouts  53.4 us (5%)
  other arithmetic  41.6 us (4%)
  starting transfers between devices  40.1 us (4%)
  between operations  15.7 us (1%)
    reduce_scatter x4, waiting for transfers between devices, sum_over_rows(): lax.psum_scatter(partial_term(jnp.int32(0), mine * lax.axis_size('row')),...  287 us
    unnamed x16, waiting for transfers between devices  142 us
    all_gather x4, blocking collectives, gather_cols(): return lax.all_gather(values, 'col', axis=0, tiled=True)  109 us
    all_gather x3, waiting for transfers between devices, gather_rows(): return lax.all_gather(values, 'row', axis=0, tiled=True)  80.2 us
    psum x1, waiting for transfers between devices, body(): lax.psum(qkv_grad.astype(jnp.bfloat16), 'dp').astype(jnp.float32)  55.3 us
    all_to_all x2, waiting for transfers between devices, spread_heads(): lax.all_to_all(values, 'col', split_axis=0, concat_axis=1, tiled=True)  36.8 us
    all_to_all x2, blocking collectives, collect_heads(): lax.all_to_all(values, 'col', split_axis=1, concat_axis=0, tiled=True)  34.1 us
    ppermute x16, starting transfers between devices, shifted(): return lax.ppermute(array, axis, pairs)  30.3 us
  transfers between devices with their start and end apart: 30, of which 16 were waited for; matrix products, arithmetic and copies ran while one was open for 11% of the time, Pallas kernels for 0%

commit v1 on v0

v1 whole, which is shorter than its diff:
```python
import jax
import jax.numpy as jnp
from jax import lax
from jax.sharding import PartitionSpec as P

HEADS = 14
KV_HEADS = 2
HEAD_DIM = 64
REACH = 8


norm_eps = 1e-06
rope_base = 1000000.0
masked_score = -1e30

bf16 = jnp.bfloat16
f32 = jnp.float32


def swap(array, axis, flip):
    count = lax.axis_size(axis)
    return lax.ppermute(array, axis, [(i, i ^ flip) for i in range(count)])


def shifted(array, axis, by):
    count = lax.axis_size(axis)
    pairs = [(i, i + by) for i in range(count) if 0 <= i + by < count]
    return lax.ppermute(array, axis, pairs)


def pick(array, index):
    return lax.dynamic_index_in_dim(array, index, 0, keepdims=False)


def product(left, right):
    return jnp.dot(left, right, preferred_element_type=f32)


def product_t(left, right):
    return lax.dot_general(left, right, (((1,), (1,)), ((), ())), preferred_element_type=f32)


def contract_rows(left, right):
    return lax.dot_general(left, right, (((0,), (0,)), ((), ())), preferred_element_type=f32)


def kept(values):
    return lax.optimization_barrier(values.astype(bf16))


def gather_row(block):
    other = swap(block, "row", 2)
    return [block, swap(block, "row", 1), other, swap(other, "row", 1)]


def scatter_row(blocks):
    near = swap(jnp.concatenate([blocks[1], blocks[3]], 0), "row", 1)
    rows = blocks[0].shape[0]
    mine = blocks[0].astype(f32) + near[:rows].astype(f32)
    away = blocks[2].astype(f32) + near[rows:].astype(f32)
    away = kept(away)
    return kept(mine).astype(f32) + swap(away, "row", 2).astype(f32)


def scatter_col(pieces, place):
    own = pick(pieces, place).astype(f32)
    got = [swap(pick(pieces, place ^ flip), "col", flip).astype(f32) for flip in (3, 2, 1)]
    return (own + got[2]) + (got[1] + got[0])


def over_groups(values):
    low = kept(values)
    if lax.axis_size("dp") == 2:
        return low.astype(f32) + swap(low, "dp", 1).astype(f32)
    return lax.psum(low, "dp").astype(f32)


def exchange_row(blocks):
    return [blocks[0]] + [swap(blocks[k], "row", k) for k in (1, 2, 3)]


def locate(indices, lengths):
    ends = jnp.cumsum(lengths)
    starts = ends - lengths
    segment = jnp.sum((indices[:, None] >= ends[None, :]).astype(jnp.int32), 1)
    chosen = segment[:, None] == jnp.arange(lengths.shape[0], dtype=jnp.int32)[None, :]
    position = indices - jnp.sum(jnp.where(chosen, starts[None, :], 0), 1)
    return (segment, position)


def rope_tables(position):
    half = HEAD_DIM // 2
    rates = rope_base ** (-(jnp.arange(half, dtype=f32) * 2.0) / HEAD_DIM)
    angles = position.astype(f32)[:, None] * rates[None, :]
    cosine = jnp.cos(angles)
    sine = jnp.sin(angles)
    return (jnp.concatenate([cosine, cosine], -1), jnp.concatenate([sine, sine], -1))


def rotate(values, cosine, sine):
    half = values.shape[-1] // 2
    turned = jnp.concatenate([-values[..., half:], values[..., :half]], -1)
    return values * cosine[:, None, :] + turned * sine[:, None, :]


def rotate_back(grads, cosine, sine):
    half = grads.shape[-1] // 2
    moved = grads * sine[:, None, :]
    turned = jnp.concatenate([moved[..., half:], -moved[..., :half]], -1)
    return grads * cosine[:, None, :] + turned


def score_block(group_queries, group_keys, allowed, scale):
    scores = (
        jnp.einsum("qha,ka->hqk", group_queries, group_keys, preferred_element_type=f32) * scale
    )
    return jnp.where(allowed[None], scores, masked_score)


def three_parts(values):
    high = lax.reduce_precision(values, 8, 7)
    rest = values - high
    middle = lax.reduce_precision(rest, 8, 7)
    return [high.astype(bf16), middle.astype(bf16), (rest - middle).astype(bf16)]


def body(
    hidden_in,
    norm1_gain,
    qkv_weight,
    qkv_bias,
    out_weight,
    norm2_gain,
    gate_weight,
    up_weight,
    down_weight,
    seq_lens,
    out_grad,
):
    row_count = lax.axis_size("row")
    col_count = lax.axis_size("col")
    row_place = lax.axis_index("row")
    col_place = lax.axis_index("col")
    quarter, part = hidden_in.shape
    block = quarter // row_count
    width = part * row_count
    lengths = seq_lens[0]
    group_heads = HEADS // KV_HEADS
    scale = HEAD_DIM ** (-0.5)
    query_width = HEADS * HEAD_DIM
    kv_width = KV_HEADS * HEAD_DIM
    qkv_cols = qkv_weight.shape[1]
    out_cols = out_weight.shape[0]
    flips = range(row_count)

    both = jnp.concatenate([hidden_in, out_grad], 1).reshape(row_count, block, 2 * part)
    both = exchange_row([pick(both, row_place ^ k) for k in flips])
    inputs_low = jnp.concatenate([b[:, :part] for b in both], 1)
    upstream_low = jnp.concatenate([b[:, part:] for b in both], 1)
    inputs = inputs_low.astype(f32)
    upstream = upstream_low.astype(f32)

    spare = 16
    first_rows = jnp.concatenate([qkv_weight, out_weight.T], 1)
    bias_row = jnp.pad(qkv_bias[None, :], ((0, spare - 1), (0, out_cols)))
    attn_cols = lax.all_gather(jnp.concatenate([first_rows, bias_row], 0), "col", axis=0)
    attn_block = jnp.concatenate(
        [attn_cols[c, :part, :qkv_cols] for c in range(col_count)]
        + [attn_cols[c, :part, qkv_cols:] for c in range(col_count)],
        1,
    )
    bias = jnp.concatenate([attn_cols[c, part, :qkv_cols] for c in range(col_count)], 0)
    gain_rows = jnp.stack(three_parts(norm1_gain) + three_parts(norm2_gain), 0)
    gain_rows = jnp.pad(gain_rows, ((0, spare - 6), (0, attn_block.shape[1] - part)))
    attn_blocks = gather_row(jnp.concatenate([attn_block, gain_rows], 0))
    qkv_wide = query_width + 2 * kv_width
    qkv_full = jnp.concatenate([b[:part, :qkv_wide] for b in attn_blocks], 0)
    out_full_t = jnp.concatenate([b[:part, qkv_wide:] for b in attn_blocks], 0)
    gains = jnp.concatenate([b[part : part + 6, :part] for b in attn_blocks], 1).astype(f32)
    gain1 = gains[0] + gains[1] + gains[2]
    gain2 = gains[3] + gains[4] + gains[5]

    ff_block = jnp.concatenate([gate_weight, up_weight, down_weight.T], 0)
    ff_blocks = gather_row(ff_block)
    gate_full = jnp.concatenate([b[:part] for b in ff_blocks], 0)
    up_full = jnp.concatenate([b[part : 2 * part] for b in ff_blocks], 0)
    down_full_t = jnp.concatenate([b[2 * part :] for b in ff_blocks], 0)

    upstream_all = lax.all_gather(upstream_low, "col", axis=0, tiled=True)

    scale1 = lax.rsqrt(jnp.mean(inputs * inputs, 1, keepdims=True) + norm_eps)
    normed1 = (inputs * scale1 * gain1).astype(bf16)
    projected = product(normed1, qkv_full) + bias.astype(f32)

    place = col_place * row_count + row_place
    first = place * block
    query_index = first + jnp.arange(block, dtype=jnp.int32)
    query_segment, query_position = locate(query_index, lengths)
    cosine, sine = rope_tables(query_position)
    queries = rotate(
        projected[:, :query_width].reshape(block, HEADS, HEAD_DIM), cosine, sine
    ).astype(bf16)
    keys = rotate(
        projected[:, query_width : query_width + kv_width].reshape(block, KV_HEADS, HEAD_DIM),
        cosine,
        sine,
    )
    values = projected[:, query_width + kv_width :]
    own_pair = jnp.concatenate([keys.reshape(block, kv_width), values], 1).astype(bf16)
    spans = REACH // row_count + 1
    from_cols = jnp.concatenate(
        [own_pair] + [shifted(own_pair, "col", back) for back in range(1, spans)], 0
    )
    pairs = jnp.concatenate(gather_row(from_cols), 0).reshape(
        row_count * spans, block, 2 * kv_width
    )
    window = []
    for hop in range(REACH, -1, -1):
        their_row = (row_place - hop) % row_count
        back = (hop + their_row - row_place) // row_count
        window.append(pick(pairs, (row_place ^ their_row) * spans + back))
    window = jnp.concatenate(window, 0)
    key_index = first - REACH * block + jnp.arange((REACH + 1) * block, dtype=jnp.int32)
    key_segment = locate(key_index, lengths)[0]
    allowed = (
        (key_index[None, :] >= 0)
        & (key_segment[None, :] == query_segment[:, None])
        & (key_index[None, :] <= query_index[:, None])
    )
    attended_parts = []
    log_totals = []
    for group in range(KV_HEADS):
        group_queries = queries[:, group * group_heads : (group + 1) * group_heads]
        group_keys = window[:, group * HEAD_DIM : (group + 1) * HEAD_DIM]
        group_values = window[:, kv_width + group * HEAD_DIM : kv_width + (group + 1) * HEAD_DIM]
        scores = score_block(group_queries, group_keys, allowed, scale)
        top = jnp.max(scores, -1, keepdims=True)
        raised = jnp.exp(scores - top)
        total = jnp.sum(raised, -1, keepdims=True)
        weights = (raised / total).astype(bf16)
        attended_parts.append(
            jnp.einsum("hqk,ka->qha", weights, group_values, preferred_element_type=f32)
        )
        log_totals.append(top + jnp.log(total))
    attended = jnp.concatenate(attended_parts, 1).reshape(block, query_width).astype(bf16)

    middle = inputs + product_t(attended, out_full_t)
    scale2 = lax.rsqrt(jnp.mean(middle * middle, 1, keepdims=True) + norm_eps)
    normed2 = (middle * scale2 * gain2).astype(bf16)
    normed2_all = lax.all_gather(normed2, "col", axis=0, tiled=True)

    gate = product(normed2_all, gate_full)
    up = product(normed2_all, up_full)
    grad_hidden = product(upstream_all, down_full_t)
    sigma = jax.nn.sigmoid(gate)
    hidden = (gate * sigma * up).astype(bf16)
    grad_gate = (grad_hidden * up * sigma * (1.0 + gate * (1.0 - sigma))).astype(bf16)
    grad_up = (grad_hidden * gate * sigma).astype(bf16)
    grad_normed2 = (product_t(grad_gate, gate_full) + product_t(grad_up, up_full)).astype(bf16)
    grad_normed2 = scatter_col(grad_normed2.reshape(col_count, block, width), col_place)

    layer_out = product_t(hidden, down_full_t).astype(bf16)
    layer_out = scatter_col(layer_out.reshape(col_count, block, width), col_place)
    hidden_out = (middle + layer_out).astype(bf16)
    hidden_out = exchange_row([hidden_out[:, k * part : (k + 1) * part] for k in flips])

    def ff_grad(left, right):
        whole = contract_rows(left, right).astype(bf16)
        mine = scatter_row([whole[k * part : (k + 1) * part] for k in flips])
        return over_groups(mine)

    down_grad = ff_grad(upstream_all, hidden).T
    gate_grad = ff_grad(normed2_all, grad_gate)
    up_grad = ff_grad(normed2_all, grad_up)

    gain2_grad = jnp.sum(grad_normed2 * middle * scale2, 0)
    scaled2 = grad_normed2 * gain2
    middle_sum = jnp.sum(scaled2 * middle, 1, keepdims=True)
    grad_middle = upstream + scale2 * scaled2 - middle * (scale2**3 * middle_sum / width)
    middle_low = grad_middle.astype(bf16)
    grad_attended = product(middle_low, out_full_t).astype(bf16)
    out_t_grad = contract_rows(middle_low, attended).astype(bf16)

    grad_heads = grad_attended.reshape(block, HEADS, HEAD_DIM)
    query_grads = []
    key_grads = []
    value_grads = []
    for group in range(KV_HEADS):
        group_queries = queries[:, group * group_heads : (group + 1) * group_heads]
        group_keys = window[:, group * HEAD_DIM : (group + 1) * HEAD_DIM]
        group_values = window[:, kv_width + group * HEAD_DIM : kv_width + (group + 1) * HEAD_DIM]
        group_grads = grad_heads[:, group * group_heads : (group + 1) * group_heads]
        scores = score_block(group_queries, group_keys, allowed, scale)
        probs = jnp.exp(scores - log_totals[group])
        grad_probs = jnp.einsum(
            "qha,ka->hqk", group_grads, group_values, preferred_element_type=f32
        )
        grad_scores = (
            probs * (grad_probs - jnp.sum(probs * grad_probs, -1, keepdims=True))
        ).astype(bf16)
        query_grads.append(
            jnp.einsum("hqk,ka->qha", grad_scores, group_keys, preferred_element_type=f32) * scale
        )
        key_grads.append(
            jnp.einsum("hqk,qha->ka", grad_scores, group_queries, preferred_element_type=f32)
            * scale
        )
        value_grads.append(
            jnp.einsum("hqk,qha->ka", probs.astype(bf16), group_grads, preferred_element_type=f32)
        )
    grad_window = jnp.concatenate(key_grads + value_grads, 1).astype(bf16)
    grad_window = grad_window.reshape(REACH + 1, block, 2 * kv_width)
    grad_blocks = []
    for flip in flips:
        pieces = []
        for back in range(spans):
            hop = back * row_count + row_place - (row_place ^ flip)
            inside = (hop >= 0) & (hop <= REACH)
            piece = pick(grad_window, jnp.clip(REACH - hop, 0, REACH))
            pieces.append(jnp.where(inside, piece, jnp.zeros_like(piece)))
        grad_blocks.append(jnp.concatenate(pieces, 0))
    grad_pairs = scatter_row(grad_blocks).reshape(spans, block, 2 * kv_width)
    grad_pair = grad_pairs[0]
    for back in range(1, spans):
        grad_pair = grad_pair + shifted(kept(grad_pairs[back]), "col", -back).astype(f32)

    grad_queries = rotate_back(jnp.concatenate(query_grads, 1), cosine, sine)
    grad_keys = rotate_back(
        grad_pair[:, :kv_width].reshape(block, KV_HEADS, HEAD_DIM), cosine, sine
    )
    grad_projected = jnp.concatenate(
        [
            grad_queries.reshape(block, query_width),
            grad_keys.reshape(block, kv_width),
            grad_pair[:, kv_width:],
        ],
        1,
    ).astype(bf16)
    grad_normed1 = product_t(grad_projected, qkv_full)
    gain1_grad = jnp.sum(grad_normed1 * inputs * scale1, 0)
    scaled1 = grad_normed1 * gain1
    input_sum = jnp.sum(scaled1 * inputs, 1, keepdims=True)
    hidden_grad = grad_middle + scale1 * scaled1 - inputs * (scale1**3 * input_sum / width)
    hidden_grad = exchange_row([hidden_grad[:, k * part : (k + 1) * part] for k in flips])

    out_mine = scatter_row([out_t_grad[k * part : (k + 1) * part] for k in flips])
    out_mine = kept(out_mine).reshape(part, col_count, out_cols).swapaxes(0, 1)
    out_w_grad = over_groups(scatter_col(out_mine, col_place)).T

    qkv_grad = contract_rows(normed1, grad_projected).astype(bf16)
    bias_sums = jnp.sum(grad_projected.astype(f32), 0)
    qkv_blocks = []
    for k in flips:
        extra = [bias_sums]
        for sums in (gain1_grad, gain2_grad):
            sums = jnp.pad(sums[k * part : (k + 1) * part], (0, qkv_cols - part))
            extra.append(jnp.tile(sums, col_count))
        extra = jnp.pad(jnp.stack(extra, 0), ((0, spare - len(extra)), (0, 0))).astype(bf16)
        qkv_blocks.append(jnp.concatenate([qkv_grad[k * part : (k + 1) * part], extra], 0))
    qkv_mine = scatter_row(qkv_blocks)
    qkv_mine = kept(qkv_mine).reshape(part + spare, col_count, qkv_cols).swapaxes(0, 1)
    qkv_mine = over_groups(scatter_col(qkv_mine, col_place))

    return (
        jnp.concatenate(_in_order(hidden_out, row_place), 0),
        jnp.concatenate(_in_order(hidden_grad, row_place), 0),
        qkv_mine[part + 1, :part],
        qkv_mine[:part],
        qkv_mine[part],
        out_w_grad,
        qkv_mine[part + 2, :part],
        gate_grad,
        up_grad,
        down_grad,
    )


def _in_order(blocks, place):
    stacked = jnp.stack(blocks, 0)
    return [pick(stacked, place ^ k) for k in range(len(blocks))]


def solution(mesh):
    return jax.shard_map(
        body,
        mesh=mesh,
        in_specs=(
            P(("dp", "col"), "row"),
            P("row"),
            P("row", "col"),
            P("col"),
            P("col", "row"),
            P("row"),
            P("row", "col"),
            P("row", "col"),
            P("col", "row"),
            P("dp", None),
            P(("dp", "col"), "row"),
        ),
        out_specs=(
            P(("dp", "col"), "row"),
            P(("dp", "col"), "row"),
            P("row"),
            P("row", "col"),
            P("col"),
            P("col", "row"),
            P("row"),
            P("row", "col"),
            P("row", "col"),
            P("col", "row"),
        ),
        check_vma=False,
    )
```

time: 1050 us -> 460 us (0.44)
  waiting for transfers between devices: 609 us -> 133 us
  blocking collectives: 207 us -> 68 us
  local copies, waits for them, and re-layouts: 53.4 us -> 98.4 us
  matrix products: 77.6 us -> 52.9 us
  between operations: 15.7 us -> 3.64 us
    reduce_scatter x4 -> x0, waiting for transfers between devices: 287 us -> none  [sum_over_rows(): lax.psum_scatter(partial_term(jnp.int32(0), mine * lax.axis_size('row')),...]
    unnamed x16 -> x0, waiting for transfers between devices: 142 us -> none
    ppermute x0 -> x47, waiting for transfers between devices: none -> 129 us  [swap(): return lax.ppermute(array, axis, [(i, i ^ flip) for i in range(count)])]
    all_gather x3 -> x0, waiting for transfers between devices: 80.2 us -> none  [gather_rows(): return lax.all_gather(values, 'row', axis=0, tiled=True)]
    psum x1 -> x0, waiting for transfers between devices: 55.3 us -> none  [body(): lax.psum(qkv_grad.astype(jnp.bfloat16), 'dp').astype(jnp.float32)]
    psum x6 -> x0, blocking collectives: 54.4 us -> none  [the longest x4 28.6 us: feature_total(): return lax.psum(values, 'row')]
    all_gather x5 -> x3, blocking collectives: 118 us -> 68 us  [the longest x1 23.5 us: body(): lax.all_gather(jnp.concatenate([first_rows, bias_row], 0), 'col', axis=0)]
    ppermute x0 -> x47, starting transfers between devices: none -> 36.9 us  [swap(): return lax.ppermute(array, axis, [(i, i ^ flip) for i in range(count)])]
  transfers between devices with their start and end apart: 30 -> 51, of which waited for: 16 -> 17; matrix products, arithmetic and copies ran while one was open for 11% -> 36% of each run, Pallas kernels for 0% -> 0%
where the time goes in v1:
time: 460 us; the launch traced here: 453 us
  waiting for transfers between devices  133 us (29%)
  local copies, waits for them, and re-layouts  98.4 us (21%)
  blocking collectives  68 us (15%)
  matrix products  52.9 us (12%)
  other arithmetic  49.1 us (11%)
  starting transfers between devices  47.7 us (10%)
    ppermute x47, waiting for transfers between devices, swap(): return lax.ppermute(array, axis, [(i, i ^ flip) for i in range(count)])  129 us
    ppermute x47, starting transfers between devices, swap(): return lax.ppermute(array, axis, [(i, i ^ flip) for i in range(count)])  36.9 us
    all_gather x1, blocking collectives, body(): lax.all_gather(jnp.concatenate([first_rows, bias_row], 0), 'col', axis=0)  23.5 us
    all_gather x1, blocking collectives, body(): upstream_all = lax.all_gather(upstream_low, 'col', axis=0, tiled=True)  23 us
    all_gather x1, blocking collectives, body(): normed2_all = lax.all_gather(normed2, 'col', axis=0, tiled=True)  21.5 us
    unnamed x246, local copies, waits for them, and re-layouts  18.7 us
    convert_element_type x13, other arithmetic, kept(): return lax.optimization_barrier(values.astype(bf16))  15.6 us
    dot_general x5, matrix products, contract_rows(): lax.dot_general(left, right, (((0,), (0,)), ((), ())), preferred_element_...  12.1 us
  transfers between devices with their start and end apart: 51, of which 17 were waited for; matrix products, arithmetic and copies ran while one was open for 36% of the time, Pallas kernels for 0%

profile of v1, /device:TPU:0, one launch (start us, length us, event | category | flops | bytes accessed | tf_op | source)
XLA Modules:
  0.0 453.1 jit_solution(4499662307406201127)
XLA Ops:
  3.5 23.5 %all-gather = bf16[960,512]{1,0:T(8,128)(2,1)S(1)} all-gather(bf16[240,512]{1,0:T(8,128)(2,1)S(1)} %fusion.75), channel_id=2, replica_groups=mesh['dp'=2,'row'=4,'col'=4] {'col'}, dimensions={0}, use_global_device_ids=true | all-gather | bytes 1228800 | tf_op jit(solution)/shard_map/all_gather | solution.py:166
  38.9 51.7 %collective-permute-done.2 = bf16[144,448]{1,0:T(8,128)(2,1)S(1)} collective-permute-done((bf16[144,448]{1,0:T(8,128)(2,1)S(1)}, bf16[144,448]{1,0:T(8,128)(2,1)S(1)}, u32[]{:S(2)}, u32[]{:S(2)}) %collective-permute-start.2) | collective-permute-done | bytes 129056 | tf_op jit(solution)/shard_map/ppermute | solution.py:22
  91.2 5.9 %collective-permute-done.1 = bf16[144,448]{1,0:T(8,128)(2,1)S(1)} collective-permute-done((bf16[144,448]{1,0:T(8,128)(2,1)S(1)}, bf16[144,448]{1,0:T(8,128)(2,1)S(1)}, u32[]{:S(2)}, u32[]{:S(2)}) %collective-permute-start.1) | collective-permute-done | bytes 129056 | tf_op jit(solution)/shard_map/ppermute | solution.py:22
  99.3 23.0 %all_gather.15 = bf16[576,896]{1,0:T(8,128)(2,1)S(1)} all-gather(bf16[144,896]{1,0:T(8,128)(2,1)S(1)} %pad_maximum_fusion.28), channel_id=1, replica_groups=mesh['dp'=2,'row'=4,'col'=4] {'col'}, dimensions={0}, use_global_device_ids=true | all-gather | bytes 1290240 | tf_op jit(solution)/shard_map/all_gather | solution.py:189
  130.0 2.6 fusion.120
  132.6 2.7 fusion.119
  138.6 2.5 collective-permute-start.6
  141.1 5.4 %collective-permute-start.7 = (bf16[144,256]{1,0:T(8,128)(2,1)}, bf16[144,256]{1,0:T(8,128)(2,1)}, u32[]{:S(2)}, u32[]{:S(2)}) collective-permute-start(bf16[144,256]{1,0:T(8,128)(2,1)} %get-tuple-element.191), channel_id=1, source_target_pairs={{0,2},{1,3},{4,6},{5,7},{8,10},{9,11},{12,14},{13,15},{16,18},{17,... | collective-permute-start | bytes 221192 | tf_op jit(solution)/shard_map/ppermute | solution.py:28
  151.4 5.6 %collective-permute-done.9 = bf16[432,256]{1,0:T(8,128)(2,1)S(1)} collective-permute-done((bf16[432,256]{1,0:T(8,128)(2,1)S(1)}, bf16[432,256]{1,0:T(8,128)(2,1)S(1)}, u32[]{:S(2)}, u32[]{:S(2)}) %collective-permute-start.9) | collective-permute-done | bytes 221216 | tf_op jit(solution)/shard_map/ppermute | solution.py:22
  171.5 21.5 %all_gather.14 = bf16[576,896]{1,0:T(8,128)(2,1)S(1)} all-gather(bf16[144,896]{1,0:T(8,128)(2,1)S(1)} %multiply_convert_fusion.3), channel_id=1, replica_groups=mesh['dp'=2,'row'=4,'col'=4] {'col'}, dimensions={0}, use_global_device_ids=true | all-gather | bytes 1290240 | tf_op jit(solution)/shard_map/all_gather | solution.py:250
  198.1 3.6 multiply_convert_fusion.1
  203.4 3.4 convolution_convert_fusion.1
  210.7 3.5 convolution_convert_fusion.2
  217.0 2.4 collective-permute-start.22
  222.3 2.4 collective-permute-start.16
  235.6 19.9 %collective-permute-done.21 = bf16[144,896]{1,0:T(8,128)(2,1)} collective-permute-done((bf16[144,896]{1,0:T(8,128)(2,1)}, bf16[144,896]{1,0:T(8,128)(2,1)}, u32[]{:S(2)}, u32[]{:S(2)}) %collective-permute-start.21) | collective-permute-done | bytes 258080 | tf_op jit(solution)/shard_map/ppermute | solution.py:22
  257.2 6.9 %collective-permute-done.15 = bf16[144,896]{1,0:T(8,128)(2,1)S(1)} collective-permute-done((bf16[144,896]{1,0:T(8,128)(2,1)}, bf16[144,896]{1,0:T(8,128)(2,1)S(1)}, u32[]{:S(2)}, u32[]{:S(2)}) %collective-permute-start.15) | collective-permute-done | bytes 258080 | tf_op jit(solution)/shard_map/ppermute | solution.py:22
  268.9 4.5 fusion.28
  273.4 4.2 fusion
  305.2 6.1 %collective-permute-done.24 = bf16[432,256]{1,0:T(8,128)(2,1)S(1)} collective-permute-done((bf16[432,256]{1,0:T(8,128)(2,1)S(1)}, bf16[432,256]{1,0:T(8,128)(2,1)S(1)}, u32[]{:S(2)}, u32[]{:S(2)}) %collective-permute-start.24) | collective-permute-done | bytes 221216 | tf_op jit(solution)/shard_map/ppermute | solution.py:22
  316.6 3.8 collective-permute-done.26
  324.1 3.2 fusion.62
  327.6 2.3 convolution_convert_fusion.3
  349.1 2.3 copy.255
  351.4 2.9 add_convert_fusion.3
  375.0 7.0 %collective-permute-done.39 = bf16[224,224]{0,1:T(8,128)(2,1)} collective-permute-done((bf16[224,224]{0,1:T(8,128)(2,1)}, bf16[224,224]{0,1:T(8,128)(2,1)}, u32[]{:S(2)}, u32[]{:S(2)}) %collective-permute-start.39) | collective-permute-done | bytes 100384 | tf_op jit(solution)/shard_map/ppermute | solution.py:22
  394.7 6.5 %collective-permute-done.43 = bf16[224,1216]{1,0:T(8,128)(2,1)} collective-permute-done((bf16[224,1216]{1,0:T(8,128)(2,1)}, bf16[224,1216]{1,0:T(8,128)(2,1)}, u32[]{:S(2)}, u32[]{:S(2)}) %collective-permute-start.43) | collective-permute-done | bytes 544800 | tf_op jit(solution)/shard_map/ppermute | solution.py:22
  406.0 2.8 add_convert_fusion.12
  411.7 5.0 %collective-permute-done.47 = bf16[224,1216]{1,0:T(8,128)(2,1)} collective-permute-done((bf16[224,1216]{1,0:T(8,128)(2,1)}, bf16[224,1216]{1,0:T(8,128)(2,1)}, u32[]{:S(2)}, u32[]{:S(2)}) %collective-permute-start.47) | collective-permute-done | bytes 544800 | tf_op jit(solution)/shard_map/ppermute | solution.py:22
  429.1 2.8 collective-permute-start.34
  435.2 2.8 collective-permute-done.34
  438.1 4.7 %collective-permute-done.33 = bf16[240,288]{0,1:T(8,128)(2,1)} collective-permute-done((bf16[240,288]{0,1:T(8,128)(2,1)S(1)}, bf16[240,288]{0,1:T(8,128)(2,1)}, u32[]{:S(2)}, u32[]{:S(2)}) %collective-permute-start.33) | collective-permute-done | bytes 138272 | tf_op jit(solution)/shard_map/ppermute | solution.py:22
  (569 shorter events, 201.9 us)
Async XLA Ops:
  30.7 91.5 %collective-permute-start.4 = (bf16[240,2048]{1,0:T(8,128)(2,1)}, bf16[240,2048]{1,0:T(8,128)(2,1)}, u32[]{:S(2)}, u32[]{:S(2)}) collective-permute-start(bf16[240,2048]{1,0:T(8,128)(2,1)} %fusion.49), channel_id=1, source_target_pairs={{0,8},{4,12},{8,0},{12,4},{1,9},{5,13},{9,1},{13,5},{2,10},{6,14},... | collective-permute-start | bytes 2949128 | tf_op jit(solution)/shard_map/ppermute | solution.py:22
  32.3 93.6 %collective-permute-start.3 = (bf16[240,2048]{1,0:T(8,128)(2,1)}, bf16[240,2048]{1,0:T(8,128)(2,1)}, u32[]{:S(2)}, u32[]{:S(2)}) collective-permute-start(bf16[240,2048]{1,0:T(8,128)(2,1)} %fusion.49), channel_id=1, source_target_pairs={{0,4},{4,0},{8,12},{12,8},{1,5},{5,1},{9,13},{13,9},{2,6},{6,2},{1... | collective-permute-start | bytes 2949128 | tf_op jit(solution)/shard_map/ppermute | solution.py:22
  33.7 95.8 %collective-permute-start.12 = (bf16[672,1216]{1,0:T(8,128)(2,1)}, bf16[672,1216]{1,0:T(8,128)(2,1)}, u32[]{:S(2)}, u32[]{:S(2)}) collective-permute-start(bf16[672,1216]{1,0:T(8,128)(2,1)} %pad_maximum_fusion.4), channel_id=1, source_target_pairs={{0,8},{4,12},{8,0},{12,4},{1,9},{5,13},{9,1},{13,5},{2,10},{6,14},... | collective-permute-start | bytes 4902920 | tf_op jit(solution)/shard_map/ppermute | solution.py:22
  34.2 98.4 %collective-permute-start.11 = (bf16[672,1216]{1,0:T(8,128)(2,1)}, bf16[672,1216]{1,0:T(8,128)(2,1)}, u32[]{:S(2)}, u32[]{:S(2)}) collective-permute-start(bf16[672,1216]{1,0:T(8,128)(2,1)} %pad_maximum_fusion.4), channel_id=1, source_target_pairs={{0,4},{4,0},{8,12},{12,8},{1,5},{5,1},{9,13},{13,9},{2,6},{6,2},{1... | collective-permute-start | bytes 4902920 | tf_op jit(solution)/shard_map/ppermute | solution.py:22
  35.1 55.5 %collective-permute-start.2 = (bf16[144,448]{1,0:T(8,128)(2,1)S(1)}, bf16[144,448]{1,0:T(8,128)(2,1)S(1)}, u32[]{:S(2)}, u32[]{:S(2)}) collective-permute-start(bf16[144,448]{1,0:T(8,128)(2,1)S(1)} %get-tuple-element.152), channel_id=1, source_target_pairs={{0,12},{4,8},{8,4},{12,0},{1,13},{5,9},{9,5},{13,1},{2,14},{6,10},... | collective-permute-start | bytes 387080 | tf_op jit(solution)/shard_map/ppermute | solution.py:22
  129.4 63.6 %collective-permute-start.13 = (bf16[672,1216]{1,0:T(8,128)(2,1)}, bf16[672,1216]{1,0:T(8,128)(2,1)}, u32[]{:S(2)}, u32[]{:S(2)}) collective-permute-start(bf16[672,1216]{1,0:T(8,128)(2,1)} %collective-permute-done.12), channel_id=1, source_target_pairs={{0,4},{4,0},{8,12},{12,8},{1,5},{5,1},{9,13},{13,9},{2,6},{6,2},{1... | collective-permute-start | bytes 4902920 | tf_op jit(solution)/shard_map/ppermute | solution.py:22
  217.0 18.3 %collective-permute-start.20 = (bf16[144,896]{1,0:T(8,128)(2,1)}, bf16[144,896]{1,0:T(8,128)(2,1)}, u32[]{:S(2)}, u32[]{:S(2)}) collective-permute-start(bf16[144,896]{1,0:T(8,128)(2,1)} %get-tuple-element.111), channel_id=1, source_target_pairs={{0,1},{1,0},{2,3},{3,2},{4,5},{5,4},{6,7},{7,6},{8,9},{9,8},{10,11... | collective-permute-start | bytes 774152 | tf_op jit(solution)/shard_map/ppermute | solution.py:22
  217.0 18.7 %collective-permute-start.22 = (bf16[144,896]{1,0:T(8,128)(2,1)}, bf16[144,896]{1,0:T(8,128)(2,1)}, u32[]{:S(2)}, u32[]{:S(2)}) collective-permute-start(bf16[144,896]{1,0:T(8,128)(2,1)} %get-tuple-element.112), channel_id=1, source_target_pairs={{0,3},{1,2},{2,1},{3,0},{4,7},{5,6},{6,5},{7,4},{8,11},{9,10},{10,... | collective-permute-start | bytes 774152 | tf_op jit(solution)/shard_map/ppermute | solution.py:22
  219.3 36.2 %collective-permute-start.21 = (bf16[144,896]{1,0:T(8,128)(2,1)}, bf16[144,896]{1,0:T(8,128)(2,1)}, u32[]{:S(2)}, u32[]{:S(2)}) collective-permute-start(bf16[144,896]{1,0:T(8,128)(2,1)} %get-tuple-element.113), channel_id=1, source_target_pairs={{0,2},{1,3},{2,0},{3,1},{4,6},{5,7},{6,4},{7,5},{8,10},{9,11},{10,... | collective-permute-start | bytes 774152 | tf_op jit(solution)/shard_map/ppermute | solution.py:22
  221.4 35.8 %collective-permute-start.14 = (bf16[144,896]{1,0:T(8,128)(2,1)}, bf16[144,896]{1,0:T(8,128)(2,1)}, u32[]{:S(2)}, u32[]{:S(2)}) collective-permute-start(bf16[144,896]{1,0:T(8,128)(2,1)} %get-tuple-element.114), channel_id=1, source_target_pairs={{0,1},{1,0},{2,3},{3,2},{4,5},{5,4},{6,7},{7,6},{8,9},{9,8},{10,11... | collective-permute-start | bytes 774152 | tf_op jit(solution)/shard_map/ppermute | solution.py:22
  222.3 34.9 %collective-permute-start.16 = (bf16[144,896]{1,0:T(8,128)(2,1)}, bf16[144,896]{1,0:T(8,128)(2,1)}, u32[]{:S(2)}, u32[]{:S(2)}) collective-permute-start(bf16[144,896]{1,0:T(8,128)(2,1)} %get-tuple-element.115), channel_id=1, source_target_pairs={{0,3},{1,2},{2,1},{3,0},{4,7},{5,6},{6,5},{7,4},{8,11},{9,10},{10,... | collective-permute-start | bytes 774152 | tf_op jit(solution)/shard_map/ppermute | solution.py:22
  235.3 28.8 %collective-permute-start.15 = (bf16[144,896]{1,0:T(8,128)(2,1)}, bf16[144,896]{1,0:T(8,128)(2,1)S(1)}, u32[]{:S(2)}, u32[]{:S(2)}) collective-permute-start(bf16[144,896]{1,0:T(8,128)(2,1)} %get-tuple-element.116), channel_id=1, source_target_pairs={{0,2},{1,3},{2,0},{3,1},{4,6},{5,7},{6,4},{7,5},{8,10},{9,11},{10,... | collective-permute-start | bytes 774152 | tf_op jit(solution)/shard_map/ppermute | solution.py:22
  235.6 103.7 %collective-permute-start.48 = (bf16[448,1216]{1,0:T(8,128)(2,1)}, bf16[448,1216]{1,0:T(8,128)(2,1)}, u32[]{:S(2)}, u32[]{:S(2)}) collective-permute-start(bf16[448,1216]{1,0:T(8,128)(2,1)} %copy.239), channel_id=1, source_target_pairs={{0,4},{4,0},{8,12},{12,8},{1,5},{5,1},{9,13},{13,9},{2,6},{6,2},{1... | collective-permute-start | bytes 3268616 | tf_op jit(solution)/shard_map/ppermute | solution.py:22
  255.5 86.2 %collective-permute-start.45 = (bf16[448,1216]{1,0:T(8,128)(2,1)}, bf16[448,1216]{1,0:T(8,128)(2,1)}, u32[]{:S(2)}, u32[]{:S(2)}) collective-permute-start(bf16[448,1216]{1,0:T(8,128)(2,1)} %copy.232), channel_id=1, source_target_pairs={{0,4},{4,0},{8,12},{12,8},{1,5},{5,1},{9,13},{13,9},{2,6},{6,2},{1... | collective-permute-start | bytes 3268616 | tf_op jit(solution)/shard_map/ppermute | solution.py:22
  290.1 13.2 %collective-permute-start.19 = (bf16[144,224]{1,0:T(8,128)(2,1)}, bf16[144,224]{1,0:T(8,128)(2,1)}, u32[]{:S(2)}, u32[]{:S(2)}) collective-permute-start(bf16[144,224]{1,0:T(8,128)(2,1)} %get-tuple-element.174), channel_id=1, source_target_pairs={{0,12},{4,8},{8,4},{12,0},{1,13},{5,9},{9,5},{13,1},{2,14},{6,10},... | collective-permute-start | bytes 193544 | tf_op jit(solution)/shard_map/ppermute | solution.py:22
  290.1 13.3 %collective-permute-start.18 = (bf16[144,224]{1,0:T(8,128)(2,1)}, bf16[144,224]{1,0:T(8,128)(2,1)}, u32[]{:S(2)}, u32[]{:S(2)}) collective-permute-start(bf16[144,224]{1,0:T(8,128)(2,1)} %get-tuple-element.175), channel_id=1, source_target_pairs={{0,8},{4,12},{8,0},{12,4},{1,9},{5,13},{9,1},{13,5},{2,10},{6,14},... | collective-permute-start | bytes 193544 | tf_op jit(solution)/shard_map/ppermute | solution.py:22
  303.3 42.0 %collective-permute-start.42 = (bf16[448,1216]{1,0:T(8,128)(2,1)}, bf16[448,1216]{1,0:T(8,128)(2,1)}, u32[]{:S(2)}, u32[]{:S(2)}) collective-permute-start(bf16[448,1216]{1,0:T(8,128)(2,1)} %copy.225), channel_id=1, source_target_pairs={{0,4},{4,0},{8,12},{12,8},{1,5},{5,1},{9,13},{13,9},{2,6},{6,2},{1... | collective-permute-start | bytes 3268616 | tf_op jit(solution)/shard_map/ppermute | solution.py:22
  320.4 15.5 %collective-permute-start.36 = (bf16[448,896]{1,0:T(8,128)(2,1)}, bf16[448,896]{1,0:T(8,128)(2,1)}, u32[]{:S(2)}, u32[]{:S(2)}) collective-permute-start(bf16[448,896]{1,0:T(8,128)(2,1)} %pad_maximum_fusion.10), channel_id=1, source_target_pairs={{0,4},{4,0},{8,12},{12,8},{1,5},{5,1},{9,13},{13,9},{2,6},{6,2},{1... | collective-permute-start | bytes 2408456 | tf_op jit(solution)/shard_map/ppermute | solution.py:22
  332.9 27.8 %collective-permute-start.29 = (f32[144,224]{1,0:T(8,128)}, f32[144,224]{1,0:T(8,128)}, u32[]{:S(2)}, u32[]{:S(2)}) collective-permute-start(f32[144,224]{1,0:T(8,128)} %get-tuple-element.156), channel_id=1, source_target_pairs={{0,12},{4,8},{8,4},{12,0},{1,13},{5,9},{9,5},{13,1},{2,14},{6,10},... | collective-permute-start | bytes 387080 | tf_op jit(solution)/shard_map/ppermute | solution.py:22
  335.9 26.2 %collective-permute-start.28 = (f32[144,224]{1,0:T(8,128)}, f32[144,224]{1,0:T(8,128)}, u32[]{:S(2)}, u32[]{:S(2)}) collective-permute-start(f32[144,224]{1,0:T(8,128)} %get-tuple-element.157), channel_id=1, source_target_pairs={{0,8},{4,12},{8,0},{12,4},{1,9},{5,13},{9,1},{13,5},{2,10},{6,14},... | collective-permute-start | bytes 387080 | tf_op jit(solution)/shard_map/ppermute | solution.py:22
  339.3 22.8 %collective-permute-start.27 = (f32[144,224]{1,0:T(8,128)}, f32[144,224]{1,0:T(8,128)}, u32[]{:S(2)}, u32[]{:S(2)}) collective-permute-start(f32[144,224]{1,0:T(8,128)} %get-tuple-element.158), channel_id=1, source_target_pairs={{0,4},{4,0},{8,12},{12,8},{1,5},{5,1},{9,13},{13,9},{2,6},{6,2},{1... | collective-permute-start | bytes 387080 | tf_op jit(solution)/shard_map/ppermute | solution.py:22
  341.8 64.2 %collective-permute-start.30 = (bf16[480,1152]{1,0:T(8,128)(2,1)}, bf16[480,1152]{1,0:T(8,128)(2,1)}, u32[]{:S(2)}, u32[]{:S(2)}) collective-permute-start(bf16[480,1152]{1,0:T(8,128)(2,1)} %fusion.46), channel_id=1, source_target_pairs={{0,4},{4,0},{8,12},{12,8},{1,5},{5,1},{9,13},{13,9},{2,6},{6,2},{1... | collective-permute-start | bytes 3317768 | tf_op jit(solution)/shard_map/ppermute | solution.py:22
  345.3 17.9 %collective-permute-start.37 = (bf16[224,896]{1,0:T(8,128)(2,1)}, bf16[224,896]{1,0:T(8,128)(2,1)}, u32[]{:S(2)}, u32[]{:S(2)}) collective-permute-start(bf16[224,896]{1,0:T(8,128)(2,1)} %get-tuple-element.75), channel_id=1, source_target_pairs={{0,8},{4,12},{8,0},{12,4},{1,9},{5,13},{9,1},{13,5},{2,10},{6,14},... | collective-permute-start | bytes 1204232 | tf_op jit(solution)/shard_map/ppermute | solution.py:22
  360.7 24.7 %collective-permute-start.49 = (bf16[224,1216]{1,0:T(8,128)(2,1)}, bf16[224,1216]{1,0:T(8,128)(2,1)}, u32[]{:S(2)}, u32[]{:S(2)}) collective-permute-start(bf16[224,1216]{1,0:T(8,128)(2,1)} %copy.242), channel_id=1, source_target_pairs={{0,8},{4,12},{8,0},{12,4},{1,9},{5,13},{9,1},{13,5},{2,10},{6,14},... | collective-permute-start | bytes 1634312 | tf_op jit(solution)/shard_map/ppermute | solution.py:22
  370.1 11.8 %collective-permute-start.39 = (bf16[224,224]{0,1:T(8,128)(2,1)}, bf16[224,224]{0,1:T(8,128)(2,1)}, u32[]{:S(2)}, u32[]{:S(2)}) collective-permute-start(bf16[224,224]{0,1:T(8,128)(2,1)} %bitcast.97), channel_id=1, source_target_pairs={{0,2},{1,3},{2,0},{3,1},{4,6},{5,7},{6,4},{7,5},{8,10},{9,11},{10,... | collective-permute-start | bytes 301064 | tf_op jit(solution)/shard_map/ppermute | solution.py:22
  374.3 16.3 %collective-permute-start.46 = (bf16[224,1216]{1,0:T(8,128)(2,1)}, bf16[224,1216]{1,0:T(8,128)(2,1)}, u32[]{:S(2)}, u32[]{:S(2)}) collective-permute-start(bf16[224,1216]{1,0:T(8,128)(2,1)} %copy.235), channel_id=1, source_target_pairs={{0,8},{4,12},{8,0},{12,4},{1,9},{5,13},{9,1},{13,5},{2,10},{6,14},... | collective-permute-start | bytes 1634312 | tf_op jit(solution)/shard_map/ppermute | solution.py:22
  382.0 19.2 %collective-permute-start.43 = (bf16[224,1216]{1,0:T(8,128)(2,1)}, bf16[224,1216]{1,0:T(8,128)(2,1)}, u32[]{:S(2)}, u32[]{:S(2)}) collective-permute-start(bf16[224,1216]{1,0:T(8,128)(2,1)} %copy.228), channel_id=1, source_target_pairs={{0,8},{4,12},{8,0},{12,4},{1,9},{5,13},{9,1},{13,5},{2,10},{6,14},... | collective-permute-start | bytes 1634312 | tf_op jit(solution)/shard_map/ppermute | solution.py:22
  383.8 21.4 %collective-permute-start.41 = (bf16[224,224]{0,1:T(8,128)(2,1)S(1)}, bf16[224,224]{0,1:T(8,128)(2,1)S(1)}, u32[]{:S(2)}, u32[]{:S(2)}) collective-permute-start(bf16[224,224]{0,1:T(8,128)(2,1)S(1)} %fusion.83), channel_id=1, source_target_pairs={{0,16},{16,0},{1,17},{17,1},{2,18},{18,2},{3,19},{19,3},{4,20},{20... | collective-permute-start | bytes 301064 | tf_op jit(solution)/shard_map/ppermute | solution.py:22
  388.2 21.4 %collective-permute-start.50 = (bf16[224,1216]{1,0:T(8,128)(2,1)}, bf16[224,1216]{1,0:T(8,128)(2,1)}, u32[]{:S(2)}, u32[]{:S(2)}) collective-permute-start(bf16[224,1216]{1,0:T(8,128)(2,1)} %copy.244), channel_id=1, source_target_pairs={{0,16},{16,0},{1,17},{17,1},{2,18},{18,2},{3,19},{19,3},{4,20},{20... | collective-permute-start | bytes 1634312 | tf_op jit(solution)/shard_map/ppermute | solution.py:22
  393.1 23.6 %collective-permute-start.47 = (bf16[224,1216]{1,0:T(8,128)(2,1)}, bf16[224,1216]{1,0:T(8,128)(2,1)}, u32[]{:S(2)}, u32[]{:S(2)}) collective-permute-start(bf16[224,1216]{1,0:T(8,128)(2,1)} %copy.237), channel_id=1, source_target_pairs={{0,16},{16,0},{1,17},{17,1},{2,18},{18,2},{3,19},{19,3},{4,20},{20... | collective-permute-start | bytes 1634312 | tf_op jit(solution)/shard_map/ppermute | solution.py:22
  403.7 29.4 %collective-permute-start.44 = (bf16[224,1216]{1,0:T(8,128)(2,1)}, bf16[224,1216]{1,0:T(8,128)(2,1)}, u32[]{:S(2)}, u32[]{:S(2)}) collective-permute-start(bf16[224,1216]{1,0:T(8,128)(2,1)} %copy.230), channel_id=1, source_target_pairs={{0,16},{16,0},{1,17},{17,1},{2,18},{18,2},{3,19},{19,3},{4,20},{20... | collective-permute-start | bytes 1634312 | tf_op jit(solution)/shard_map/ppermute | solution.py:22
  408.7 12.9 %collective-permute-start.31 = (bf16[240,1152]{1,0:T(8,128)(2,1)}, bf16[240,1152]{1,0:T(8,128)(2,1)}, u32[]{:S(2)}, u32[]{:S(2)}) collective-permute-start(bf16[240,1152]{1,0:T(8,128)(2,1)} %get-tuple-element.110), channel_id=1, source_target_pairs={{0,8},{4,12},{8,0},{12,4},{1,9},{5,13},{9,1},{13,5},{2,10},{6,14},... | collective-permute-start | bytes 1658888 | tf_op jit(solution)/shard_map/ppermute | solution.py:22
  (132 other events, 1756.6 us)
